TPU v7x, 256 devices: a whole 4x4x8 slice. The times are simulated.
256 devices in a mesh: chan: 64 (over z, y, core), row: 4 (over x).
Axes of the slice: x: 4, y: 4, z: 8, core: 2. Of those that a mesh axis runs over, the one named last changes fastest.
Arguments:
- generator: float32 [64, 1280, 1280], P('chan', 'row'), as said below
- hamiltonian: float32 [64, 1280, 1280], P('chan', 'row'), as said below
- recoupling: float32 [64, 1280, 1280], P('chan')
- channel_size: int32 [64], P('chan'), may hold values from 128 to 1280, as said below
- hole_first: int32 [64, 1280], P('chan'), may hold values 0 or 1
- hole_second: int32 [64, 1280], P('chan'), may hold values 0 or 1
Outputs:
- derivative: float32 [64, 1280, 1280], P('chan', 'row')
Inputs may be any that keep to these rules, and one draw needn't show every extreme that they name: generator is antisymmetric and hamiltonian symmetric in every channel block. hamiltonian is symmetric in every channel block. `channel_size`: some channel has exactly 1280 states.
All inputs are finite; a program needn't handle non-finite values. No bound on the sum of `hole_first` or of `hole_second` on one device may be relied on, other than what follows from the above.
Results may differ from a plain program's by a relative error of at most 0.000076.
Values sent between devices are 32-bit elements; how exact they have to be, the bound alone decides.
No kernel may reach another device: no remote copies, remote signals or barrier semaphores. Data moves between devices by JAX's collectives and lax.ppermute only.
A program may use at most 128 MiB of HBM per device.

v0:
```python
import jax
import jax.numpy as jnp
from jax import lax
from jax.sharding import PartitionSpec as P


def batched(left, right):
    return jnp.einsum("cij,cjk->cik", left, right, precision=lax.Precision.HIGHEST)


def shards(generator, hamiltonian, recoupling, channel_size, hole_first, hole_second):
    local_count = generator.shape[0]
    row_count = generator.shape[1]
    block_order = generator.shape[2]
    chan_count = lax.axis_size("chan")
    row_index = lax.axis_index("row")
    positions = jnp.arange(block_order, dtype=jnp.int32)
    inside = (positions[None, :] < channel_size[:, None]).astype(jnp.float32)
    row_inside = lax.dynamic_slice_in_dim(inside, row_index * row_count, row_count, 1)
    block_mask = row_inside[:, :, None] * inside[:, None, :]
    gen_live = generator * block_mask
    ham_live = hamiltonian * block_mask
    weight_pp = (1 - hole_first - hole_second).astype(jnp.float32)
    weight_ph = (hole_first - hole_second).astype(jnp.float32)
    piece_shape = (local_count, row_count, chan_count, block_order // chan_count)
    gen_moved, ham_moved = (
        lax.all_to_all(
            gen_live.reshape(piece_shape), "chan", split_axis=2, concat_axis=2, tiled=True
        ),
        lax.all_to_all(
            ham_live.reshape(piece_shape), "chan", split_axis=2, concat_axis=2, tiled=True
        ),
    )
    gen_bar = batched(gen_moved.reshape(generator.shape), recoupling)
    ham_bar = batched(ham_moved.reshape(generator.shape), recoupling)
    pieces = (
        lax.all_gather(gen_bar, "row", axis=1, tiled=True),
        lax.all_gather(ham_bar, "row", axis=1, tiled=True),
    )
    factor = weight_ph[:, None, :]
    gen_cols = gen_bar * factor
    ham_cols = ham_bar * factor
    ph_term = batched(gen_cols, pieces[1]) - batched(ham_cols, pieces[0])
    turned = jnp.einsum("cij,ckj->cik", ph_term, recoupling, precision=lax.Precision.HIGHEST)
    back_moved = lax.all_to_all(
        turned.reshape(piece_shape), "chan", split_axis=2, concat_axis=2, tiled=True
    )
    ph_back = back_moved.reshape(generator.shape)
    pieces = (
        lax.all_gather(gen_live, "row", axis=1, tiled=True),
        lax.all_gather(ham_live, "row", axis=1, tiled=True),
    )
    factor = weight_pp[:, None, :]
    gen_cols = gen_live * factor
    ham_cols = ham_live * factor
    ladder = batched(gen_cols, pieces[1]) - batched(ham_cols, pieces[0])
    return (ladder + ph_back) * block_mask


def solution(mesh):
    in_specs = (
        P("chan", "row", None),
        P("chan", "row", None),
        P("chan", None, None),
        P("chan"),
        P("chan", None),
        P("chan", None),
    )
    out_specs = P("chan", "row", None)
    return jax.shard_map(shards, mesh=mesh, in_specs=in_specs, out_specs=out_specs, check_vma=False)
```

profile of v0, /device:TPU:1, one launch (start us, length us, event | category | flops | bytes accessed | tf_op | source)
XLA Modules:
  0.0 404.9 jit_solution(18243573594442668754)
XLA Ops:
  7.2 2.2 multiply_multiply_fusion.1
  9.5 3.6 copy.20
  13.0 60.2 %all_to_all.15 = f32[1,320,64,20]{1,0,3,2:T(1,128)} all-to-all(f32[1,320,64,20]{1,0,3,2:T(1,128)} %bitcast.47), channel_id=1, replica_groups=mesh['chan'=64,'row'=4] {'chan'}, dimensions={2} | all-to-all | bytes 3276800 | tf_op jit(solution)/shard_map/all_to_all | solution.py:30
  73.2 7.7 %reduce.4 = f32[320,64,20]{0,2,1:T(8,128)} reduce(f32[1,320,64,20]{1,0,3,2:T(1,128)} %all_to_all.15, f32[]{:T(128)} %constant.18), dimensions={0}, to_apply=%all_to_all.10.reduce_sub_computation | reduce | bytes 3276804 | tf_op jit(solution)/shard_map/all_to_all | solution.py:30
  81.0 2.9 reshape.159
  83.8 11.5 %fusion = f32[320,1280]{1,0:T(8,128)} fusion(f32[320,1280]{0,1:T(8,128)} %reshape.159, f32[1,1280,1280]{2,1,0:T(8,128)} %param.8), kind=kOutput, calls=%fused_computation | convolution fusion | flops 6291456000 | bytes 9830400 | tf_op jit(solution)/shard_map/cij,cjk->cik/dot_general | solution.py:8
  95.3 0.0 all-gather.11.cloned.1.call-update
  95.3 0.0 all-gather.13.cloned.1.call-start
  95.4 3.2 copy.19
  98.6 54.1 %all_to_all.16 = f32[1,320,64,20]{1,0,3,2:T(1,128)S(1)} all-to-all(f32[1,320,64,20]{1,0,3,2:T(1,128)} %bitcast.48), channel_id=1, replica_groups=mesh['chan'=64,'row'=4] {'chan'}, dimensions={2} | all-to-all | bytes 3276800 | tf_op jit(solution)/shard_map/all_to_all | solution.py:27
  152.6 7.0 %reduce.2 = f32[320,64,20]{0,2,1:T(8,128)} reduce(f32[1,320,64,20]{1,0,3,2:T(1,128)S(1)} %all_to_all.16, f32[]{:T(128)} %constant.18), dimensions={0}, to_apply=%all_to_all.9.reduce_sub_computation | reduce | bytes 3276804 | tf_op jit(solution)/shard_map/all_to_all | solution.py:27
  159.6 2.0 reshape.156
  161.6 10.9 %fusion.2 = f32[320,1280]{1,0:T(8,128)} fusion(f32[320,1280]{0,1:T(8,128)S(1)} %reshape.156, f32[1,1280,1280]{2,1,0:T(8,128)} %param.8), kind=kOutput, calls=%fused_computation.2 | convolution fusion | flops 6291456000 | bytes 9830400 | tf_op jit(solution)/shard_map/cij,cjk->cik/dot_general | solution.py:8
  172.5 0.0 all-gather.9.cloned.1.call-start
  172.5 0.7 all-gather.9.cloned.1.call-update
  173.2 0.0 all-gather.7.cloned.1.call-start
  173.3 0.5 all-gather.7.cloned.1.call-update
  173.8 8.4 %dot_general.37 = f32[64,20,1280]{2,1,0:T(8,128)} reshape(f32[1,1280,1280]{2,1,0:T(8,128)} %param.8) | data formatting | bytes 13107200 | tf_op jit(solution)/shard_map/cij,ckj->cik/dot_general | solution.py:44
  182.3 0.0 all-gather.11.cloned.1.call-done
  182.4 11.7 %fusion.26 = f32[320,1280]{1,0:T(8,128)} fusion(f32[1280,1280]{1,0:T(8,128)} %all-gather.11.cloned.1.call-done, f32[320,1280]{1,0:T(8,128)S(1)} %copy-done.4, f32[1280]{0:T(1024)S(1)} %get-tuple-element.6), kind=kOutput, calls=%fused_computation.21 | convolution fusion | flops 6291865600 | bytes 9835520 | tf_op jit(solution)/shard_map/cij,cjk->cik/dot_general | solution.py:8
  194.0 46.6 %all-gather.13.cloned.1.call-done = f32[1280,1280]{1,0:T(8,128)} async-done(((f32[320,1280]{1,0:T(8,128)}), f32[1280,1280]{1,0:T(8,128)}) %all-gather.13.cloned.1.call-update) | async-done | bytes 6553616 | tf_op jit(solution)/shard_map/all_gather | solution.py:37
  240.6 10.5 %fusion.19 = f32[320,1280,1]{1,0,2:T(8,128)S(1)} fusion(f32[320,1280]{1,0:T(8,128)} %fusion.26, f32[1280,1280]{1,0:T(8,128)} %all-gather.13.cloned.1.call-done, f32[320,1280]{1,0:T(8,128)S(1)} %copy-done.3, f32[1280]{0:T(1024)S(1)} %get-tuple-element.6), kind=kOutput, calls=%fused_computation.14 | convolution fusion | flops 6292275200 | bytes 11473920 | tf_op jit(solution)/shard_map/cij,cjk->cik/dot_general | solution.py:8
  251.2 11.5 %fusion.30 = f32[1,320,64,20]{1,2,3,0:T(8,128)S(1)} fusion(f32[320,1280,1]{1,0,2:T(8,128)S(1)} %fusion.19, f32[64,20,1280]{2,1,0:T(8,128)S(1)} %copy-done), kind=kOutput, calls=%fused_computation.25 | convolution fusion | flops 6291456000 | bytes 9830400 | tf_op jit(solution)/shard_map/cij,ckj->cik/dot_general | solution.py:44
  262.7 3.3 copy.22
  266.0 11.0 %all-to-all-start.2 = ((f32[1,320,64,20]{1,0,3,2:T(1,128)}), f32[1,320,64,20]{1,0,3,2:T(1,128)}, u32[]{:S(2)}, u32[]{:S(2)}) async-start(f32[1,320,64,20]{1,0,3,2:T(1,128)} %copy.22), calls=%async_computation.2 | async-start | bytes 3932160 | tf_op jit(solution)/shard_map/all_to_all | solution.py:45
  277.0 36.6 %all-gather.9.cloned.1.call-done = f32[1,1280,1280]{2,1,0:T(8,128)} async-done(((f32[1,320,1280]{2,1,0:T(8,128)}), f32[1,1280,1280]{2,1,0:T(8,128)}) %all-gather.9.cloned.1.call-update) | async-done | bytes 6553616 | tf_op jit(solution)/shard_map/all_gather | solution.py:50
  313.6 10.9 %fusion.4 = f32[320,1280]{1,0:T(8,128)} fusion(f32[1,1280,1280]{2,1,0:T(8,128)} %all-gather.9.cloned.1.call-done, f32[1,320,1280]{2,1,0:T(8,128)S(1)} %copy-done.2, f32[1280]{0:T(1024)S(1)} %get-tuple-element.5), kind=kOutput, calls=%fused_computation.4 | convolution fusion | flops 6291865600 | bytes 9835520 | tf_op jit(solution)/shard_map/cij,cjk->cik/dot_general | solution.py:8
  324.5 6.3 %reduce.5 = f32[320,64,20]{0,2,1:T(8,128)S(1)} reduce(f32[1,320,64,20]{1,0,3,2:T(1,128)} %all-to-all-done.2, f32[]{:T(128)} %constant.18), dimensions={0}, to_apply=%all_to_all.11.reduce_sub_computation | reduce | bytes 3276804 | tf_op jit(solution)/shard_map/all_to_all | solution.py:45
  330.8 1.5 reshape.162
  332.3 2.3 copy.23
  334.6 51.8 %all-gather.7.cloned.1.call-done = f32[1,1280,1280]{2,1,0:T(8,128)} async-done(((f32[1,320,1280]{2,1,0:T(8,128)}), f32[1,1280,1280]{2,1,0:T(8,128)}) %all-gather.7.cloned.1.call-update) | async-done | bytes 6553616 | tf_op jit(solution)/shard_map/all_gather | solution.py:51
  386.4 11.5 %fusion.20 = f32[1,320,1280]{2,1,0:T(8,128)} fusion(f32[320,1280]{1,0:T(8,128)S(1)} %copy.23, f32[320,1280]{1,0:T(8,128)} %fusion.4, f32[1,1280,1280]{2,1,0:T(8,128)} %all-gather.7.cloned.1.call-done, f32[1280]{0:T(1024)S(1)} %fusion.37, f32[320]{0:T(512)S(1)} %fusion.38, f32[1280]{0:T(1024)S(1)} %get-tuple-element.5, f32[1,320,1280]{2,1,0:T(8,128)S(1)} %copy-done.6), kind=kOutput, calls=%fused_computation.15 | convolution fusion | flops 6294323200 | bytes 13118720 | tf_op jit(solution)/shard_map/cij,cjk->cik/dot_general | solution.py:8
  (24 shorter events, 0.1 us)
Async XLA Ops:
  6.5 175.8 %all-gather.11.cloned.1.call-start = ((), (), s32[]{:S(2)}) async-start(), calls=%async_computation.5 | async-start | bytes 8192000 | tf_op jit(solution)/shard_map/all_gather | solution.py:38
  9.4 3.6 copy-start.1
  9.5 85.9 %copy-start.5 = (f32[1,320,1280]{2,1,0:T(8,128)}, f32[1,320,1280]{2,1,0:T(8,128)S(1)}, u32[]{:S(2)}) copy-start(f32[1,320,1280]{2,1,0:T(8,128)S(1)} %get-tuple-element.7) | copy-start | bytes 4915204
  95.3 145.3 %all-gather.13.cloned.1.call-start = ((), (), s32[]{:S(2)}) async-start(), calls=%async_computation.6 | async-start | bytes 8192000 | tf_op jit(solution)/shard_map/all_gather | solution.py:37
  172.5 141.1 %all-gather.9.cloned.1.call-start = ((), (), s32[]{:S(2)}) async-start(), calls=%async_computation.4 | async-start | bytes 8192000 | tf_op jit(solution)/shard_map/all_gather | solution.py:50
  173.2 213.2 %all-gather.7.cloned.1.call-start = ((), (), s32[]{:S(2)}) async-start(), calls=%async_computation.3 | async-start | bytes 8192000 | tf_op jit(solution)/shard_map/all_gather | solution.py:51
  173.8 8.5 %copy-start.7 = (s32[1,1280]{1,0:T(1,128)S(1)}, s32[1,1280]{1,0:T(1,128)}, u32[]{:S(2)}) copy-start(s32[1,1280]{1,0:T(1,128)} %param.11) | copy-start | bytes 15364
  173.8 8.5 %copy-start.8 = (s32[1,1280]{1,0:T(1,128)S(1)}, s32[1,1280]{1,0:T(1,128)}, u32[]{:S(2)}) copy-start(s32[1,1280]{1,0:T(1,128)} %param.10) | copy-start | bytes 15364
  173.8 8.5 %copy-start.4 = (f32[320,1280]{1,0:T(8,128)S(1)}, f32[320,1280]{1,0:T(8,128)}, u32[]{:S(2)}) copy-start(f32[320,1280]{1,0:T(8,128)} %fusion.2) | copy-start | bytes 4915204
  182.4 58.2 %copy-start.3 = (f32[320,1280]{1,0:T(8,128)S(1)}, f32[320,1280]{1,0:T(8,128)}, u32[]{:S(2)}) copy-start(f32[320,1280]{1,0:T(8,128)} %fusion) | copy-start | bytes 4915204
  240.6 10.5 %copy-start = (f32[64,20,1280]{2,1,0:T(8,128)S(1)}, f32[64,20,1280]{2,1,0:T(8,128)}, u32[]{:S(2)}) copy-start(f32[64,20,1280]{2,1,0:T(8,128)} %dot_general.37) | copy-start | bytes 19660804
  266.0 47.6 %copy-start.2 = (f32[1,320,1280]{2,1,0:T(8,128)S(1)}, f32[1,320,1280]{2,1,0:T(8,128)}, u32[]{:S(2)}) copy-start(f32[1,320,1280]{2,1,0:T(8,128)} %copy-done.1) | copy-start | bytes 4915204
  266.0 58.5 %all-to-all-start.2 = ((f32[1,320,64,20]{1,0,3,2:T(1,128)}), f32[1,320,64,20]{1,0,3,2:T(1,128)}, u32[]{:S(2)}, u32[]{:S(2)}) async-start(f32[1,320,64,20]{1,0,3,2:T(1,128)} %copy.22), calls=%async_computation.2 | async-start | bytes 3932160 | tf_op jit(solution)/shard_map/all_to_all | solution.py:45
  332.3 54.2 %copy-start.6 = (f32[1,320,1280]{2,1,0:T(8,128)S(1)}, f32[1,320,1280]{2,1,0:T(8,128)}, u32[]{:S(2)}) copy-start(f32[1,320,1280]{2,1,0:T(8,128)} %param.6) | copy-start | bytes 4915204
Sparse Core Ops, SparseCore 0:
  95.4 67.9 all-gather.10
  172.6 67.9 all-gather.12
  242.4 71.1 all-gather.8
  315.3 71.1 all-gather.6
where the time goes:
time: 411 us; the launch traced here: 405 us
  waiting for transfers between devices  136 us (33%)
  blocking collectives  114 us (28%)
  matrix products  78.5 us (19%)
  local copies, waits for them, and re-layouts  27.1 us (7%)
  other arithmetic  23.3 us (6%)
  between operations  14.4 us (4%)
  starting transfers between devices  11.2 us (3%)
    dot_general x6, matrix products, batched(): jnp.einsum('cij,cjk->cik', left, right, precision=lax.Precision.HIGHEST)  66.9 us
    all_to_all x1, blocking collectives, shards(): lax.all_to_all(ham_live.reshape(piece_shape), 'chan', split_axis=2, conca...  60.2 us
    all_to_all x1, blocking collectives, shards(): lax.all_to_all(gen_live.reshape(piece_shape), 'chan', split_axis=2, conca...  54.1 us
    all_gather x1, waiting for transfers between devices, shards(): lax.all_gather(ham_live, 'row', axis=1, tiled=True)  51.8 us
    all_gather x1, waiting for transfers between devices, shards(): lax.all_gather(gen_bar, 'row', axis=1, tiled=True)  46.6 us
    all_gather x1, waiting for transfers between devices, shards(): lax.all_gather(gen_live, 'row', axis=1, tiled=True)  36.6 us
    dot_general x2, local copies, waits for them, and re-layouts, shards(): jnp.einsum('cij,ckj->cik', ph_term, recoupling, precision=lax.Precision.H...  11.7 us
    dot_general x1, matrix products, shards(): jnp.einsum('cij,ckj->cik', ph_term, recoupling, precision=lax.Precision.H...  11.5 us
  transfers between devices with their start and end apart: 5, of which 3 were waited for; matrix products, arithmetic and copies ran while one was open for 22% of the time, Pallas kernels for 0%

commit v1 on v0

--- a/solution.py
+++ b/solution.py
@@ -47,7 +47,9 @@
     )
     ph_back = back_moved.reshape(generator.shape)
     pieces = (
-        lax.all_gather(gen_live, "row", axis=1, tiled=True),
+        jnp.concatenate(
+            lax.all_to_all(jnp.stack([gen_live] * lax.axis_size("row")), "row", 0, 0), axis=1
+        ),
         lax.all_gather(ham_live, "row", axis=1, tiled=True),
     )
     factor = weight_pp[:, None, :]

time: 411 us -> 426 us (1.036)
  the two profiles are of different devices: /device:TPU:1 before, /device:TPU:4 now
where the time goes in v1:
time: 426 us; the launch traced here: 420 us
  waiting for transfers between devices  141 us (33%)
  blocking collectives  115 us (27%)
  matrix products  78.8 us (18%)
  local copies, waits for them, and re-layouts  32.3 us (8%)
  other arithmetic  25.5 us (6%)
  between operations  14.4 us (3%)
  starting transfers between devices  12.8 us (3%)
    all_gather x1, waiting for transfers between devices, shards(): lax.all_gather(gen_bar, 'row', axis=1, tiled=True)  103 us
    dot_general x6, matrix products, batched(): jnp.einsum('cij,cjk->cik', left, right, precision=lax.Precision.HIGHEST)  67.3 us
    all_to_all x1, blocking collectives, shards(): lax.all_to_all(ham_live.reshape(piece_shape), 'chan', split_axis=2, conca...  60.8 us
    all_to_all x1, blocking collectives, shards(): lax.all_to_all(gen_live.reshape(piece_shape), 'chan', split_axis=2, conca...  54.2 us
    all_to_all x1, waiting for transfers between devices, shards(): lax.all_to_all(turned.reshape(piece_shape), 'chan', split_axis=2, concat_...  37.5 us
    dot_general x2, local copies, waits for them, and re-layouts, shards(): jnp.einsum('cij,ckj->cik', ph_term, recoupling, precision=lax.Precision.H...  11.8 us
    dot_general x1, matrix products, shards(): jnp.einsum('cij,ckj->cik', ph_term, recoupling, precision=lax.Precision.H...  11.5 us
  transfers between devices with their start and end apart: 5, of which 2 were waited for; matrix products, arithmetic and copies ran while one was open for 23% of the time, Pallas kernels for 0%

profile of v1, /device:TPU:4, one launch (start us, length us, event | category | flops | bytes accessed | tf_op | source)
XLA Modules:
  0.0 420.0 jit_solution(7049729380476262008)
XLA Ops:
  7.2 2.2 multiply_multiply_fusion.1
  9.5 3.4 copy.20
  12.9 60.8 %all_to_all.20 = f32[1,320,64,20]{1,0,3,2:T(1,128)} all-to-all(f32[1,320,64,20]{1,0,3,2:T(1,128)} %bitcast.48), channel_id=1, replica_groups=mesh['chan'=64,'row'=4] {'chan'}, dimensions={2} | all-to-all | bytes 3276800 | tf_op jit(solution)/shard_map/all_to_all | solution.py:30
  73.7 7.7 %reduce.4 = f32[320,64,20]{0,2,1:T(8,128)} reduce(f32[1,320,64,20]{1,0,3,2:T(1,128)} %all_to_all.20, f32[]{:T(128)} %constant.18), dimensions={0}, to_apply=%all_to_all.14.reduce_sub_computation | reduce | bytes 3276804 | tf_op jit(solution)/shard_map/all_to_all | solution.py:30
  81.4 2.9 reshape.164
  84.3 11.5 %fusion = f32[320,1280]{1,0:T(8,128)} fusion(f32[320,1280]{0,1:T(8,128)} %reshape.164, f32[1,1280,1280]{2,1,0:T(8,128)} %param.8), kind=kOutput, calls=%fused_computation | convolution fusion | flops 6291456000 | bytes 9830400 | tf_op jit(solution)/shard_map/cij,cjk->cik/dot_general | solution.py:8
  95.8 0.0 all-gather.8.cloned.1.call-update
  95.8 0.0 all-gather.10.cloned.1.call-start
  95.8 3.2 copy.19
  99.1 54.2 %all_to_all.21 = f32[1,320,64,20]{1,0,3,2:T(1,128)} all-to-all(f32[1,320,64,20]{1,0,3,2:T(1,128)} %bitcast.49), channel_id=1, replica_groups=mesh['chan'=64,'row'=4] {'chan'}, dimensions={2} | all-to-all | bytes 3276800 | tf_op jit(solution)/shard_map/all_to_all | solution.py:27
  153.3 7.7 %reduce.2 = f32[320,64,20]{0,2,1:T(8,128)} reduce(f32[1,320,64,20]{1,0,3,2:T(1,128)} %all_to_all.21, f32[]{:T(128)} %constant.18), dimensions={0}, to_apply=%all_to_all.13.reduce_sub_computation | reduce | bytes 3276804 | tf_op jit(solution)/shard_map/all_to_all | solution.py:27
  161.0 2.9 reshape.161
  164.0 11.5 %fusion.2 = f32[320,1280]{1,0:T(8,128)} fusion(f32[320,1280]{0,1:T(8,128)} %reshape.161, f32[1,1280,1280]{2,1,0:T(8,128)} %param.8), kind=kOutput, calls=%fused_computation.2 | convolution fusion | flops 6291456000 | bytes 9830400 | tf_op jit(solution)/shard_map/cij,cjk->cik/dot_general | solution.py:8
  175.5 0.0 all-gather.6.cloned.1.call-start
  175.5 0.7 all-gather.6.cloned.1.call-update
  176.2 3.2 stack.2
  179.4 5.8 %all-to-all-start = ((f32[4,1,320,1280]{3,2,1,0:T(8,128)}), f32[4,1,320,1280]{3,2,1,0:T(8,128)}, u32[]{:S(2)}, u32[]{:S(2)}) async-start(f32[4,1,320,1280]{3,2,1,0:T(8,128)} %stack.2), calls=%async_computation | async-start | bytes 13107200 | tf_op jit(solution)/shard_map/all_to_all | solution.py:51
  185.2 8.5 %dot_general.37 = f32[64,20,1280]{2,1,0:T(8,128)} reshape(f32[1,1280,1280]{2,1,0:T(8,128)} %param.8) | data formatting | bytes 13107200 | tf_op jit(solution)/shard_map/cij,ckj->cik/dot_general | solution.py:44
  193.8 0.0 all-gather.8.cloned.1.call-done
  193.8 11.5 %fusion.25 = f32[320,1280]{1,0:T(8,128)} fusion(f32[1280,1280]{1,0:T(8,128)} %all-gather.8.cloned.1.call-done, f32[320,1280]{1,0:T(8,128)} %fusion.2, f32[1280]{0:T(1024)S(1)} %get-tuple-element.6), kind=kOutput, calls=%fused_computation.20 | convolution fusion | flops 6291865600 | bytes 9835520 | tf_op jit(solution)/shard_map/cij,cjk->cik/dot_general | solution.py:8
  205.3 102.9 %all-gather.10.cloned.1.call-done = f32[1280,1280]{1,0:T(8,128)} async-done(((f32[320,1280]{1,0:T(8,128)}), f32[1280,1280]{1,0:T(8,128)}) %all-gather.10.cloned.1.call-update) | async-done | bytes 6553616 | tf_op jit(solution)/shard_map/all_gather | solution.py:37
  308.2 10.5 %fusion.17 = f32[320,1280,1]{1,0,2:T(8,128)S(1)} fusion(f32[320,1280]{1,0:T(8,128)} %fusion.25, f32[1280,1280]{1,0:T(8,128)} %all-gather.10.cloned.1.call-done, f32[320,1280]{1,0:T(8,128)S(1)} %copy-done.3, f32[1280]{0:T(1024)S(1)} %get-tuple-element.6), kind=kOutput, calls=%fused_computation.12 | convolution fusion | flops 6292275200 | bytes 11473920 | tf_op jit(solution)/shard_map/cij,cjk->cik/dot_general | solution.py:8
  318.8 11.5 %fusion.29 = f32[1,320,64,20]{1,2,3,0:T(8,128)S(1)} fusion(f32[320,1280,1]{1,0,2:T(8,128)S(1)} %fusion.17, f32[64,20,1280]{2,1,0:T(8,128)S(1)} %copy-done), kind=kOutput, calls=%fused_computation.24 | convolution fusion | flops 6291456000 | bytes 9830400 | tf_op jit(solution)/shard_map/cij,ckj->cik/dot_general | solution.py:44
  330.3 3.3 copy.22
  333.6 7.0 %all-to-all-start.3 = ((f32[1,320,64,20]{1,0,3,2:T(1,128)}), f32[1,320,64,20]{1,0,3,2:T(1,128)}, u32[]{:S(2)}, u32[]{:S(2)}) async-start(f32[1,320,64,20]{1,0,3,2:T(1,128)} %copy.22), calls=%async_computation.3 | async-start | bytes 3932160 | tf_op jit(solution)/shard_map/all_to_all | solution.py:45
  340.6 10.9 %fusion.21 = f32[320,1280]{1,0:T(8,128)} fusion(f32[1280,1280]{1,0:T(8,128)} %bitcast.5, f32[1,320,1280]{2,1,0:T(8,128)S(1)} %copy-done.2, f32[1280]{0:T(1024)S(1)} %get-tuple-element.5), kind=kOutput, calls=%fused_computation.16 | convolution fusion | flops 6291865600 | bytes 9835520 | tf_op jit(solution)/shard_map/cij,cjk->cik/dot_general | solution.py:8
  351.5 37.5 %all-to-all-done.3 = f32[1,320,64,20]{1,0,3,2:T(1,128)} async-done(((f32[1,320,64,20]{1,0,3,2:T(1,128)}), f32[1,320,64,20]{1,0,3,2:T(1,128)}, u32[]{:S(2)}, u32[]{:S(2)}) %all-to-all-start.3) | async-done | bytes 1638432 | tf_op jit(solution)/shard_map/all_to_all | solution.py:45
  389.0 7.7 %reduce.5 = f32[320,64,20]{0,2,1:T(8,128)} reduce(f32[1,320,64,20]{1,0,3,2:T(1,128)} %all-to-all-done.3, f32[]{:T(128)} %constant.18), dimensions={0}, to_apply=%all_to_all.15.reduce_sub_computation | reduce | bytes 3276804 | tf_op jit(solution)/shard_map/all_to_all | solution.py:45
  396.8 2.7 reshape.167
  399.5 2.1 copy.23
  401.6 0.0 all-gather.6.cloned.1.call-done
  401.6 11.4 %fusion.18 = f32[1,320,1280]{2,1,0:T(8,128)} fusion(f32[320,1280]{1,0:T(8,128)S(1)} %copy.23, f32[320,1280]{1,0:T(8,128)} %fusion.21, f32[1,1280,1280]{2,1,0:T(8,128)} %all-gather.6.cloned.1.call-done, f32[1,320,1280]{2,1,0:T(8,128)S(1)} %get-tuple-element.7, f32[1280]{0:T(1024)S(1)} %fusion.36, f32[320]{0:T(512)S(1)} %fusion.37, f32[1280]{0:T(1024)S(1)} %get-tuple-element.5), kind=kOutput, calls=%fused_computation.13 | convolution fusion | flops 6293504000 | bytes 13118720 | tf_op jit(solution)/shard_map/cij,cjk->cik/dot_general | solution.py:8
  (18 shorter events, 0.1 us)
Async XLA Ops:
  6.5 187.3 %all-gather.8.cloned.1.call-start = ((), (), s32[]{:S(2)}) async-start(), calls=%async_computation.5 | async-start | bytes 8192000 | tf_op jit(solution)/shard_map/all_gather | solution.py:38
  9.4 3.5 copy-start.1
  95.8 212.4 %all-gather.10.cloned.1.call-start = ((), (), s32[]{:S(2)}) async-start(), calls=%async_computation.6 | async-start | bytes 8192000 | tf_op jit(solution)/shard_map/all_gather | solution.py:37
  175.5 226.1 %all-gather.6.cloned.1.call-start = ((), (), s32[]{:S(2)}) async-start(), calls=%async_computation.4 | async-start | bytes 8192000 | tf_op jit(solution)/shard_map/all_gather | solution.py:53
  179.4 154.2 %all-to-all-start = ((f32[4,1,320,1280]{3,2,1,0:T(8,128)}), f32[4,1,320,1280]{3,2,1,0:T(8,128)}, u32[]{:S(2)}, u32[]{:S(2)}) async-start(f32[4,1,320,1280]{3,2,1,0:T(8,128)} %stack.2), calls=%async_computation | async-start | bytes 13107200 | tf_op jit(solution)/shard_map/all_to_all | solution.py:51
  185.2 8.5 %copy-start.4 = (s32[1,1280]{1,0:T(1,128)S(1)}, s32[1,1280]{1,0:T(1,128)}, u32[]{:S(2)}) copy-start(s32[1,1280]{1,0:T(1,128)} %param.11) | copy-start | bytes 15364
  185.2 8.5 %copy-start.5 = (s32[1,1280]{1,0:T(1,128)S(1)}, s32[1,1280]{1,0:T(1,128)}, u32[]{:S(2)}) copy-start(s32[1,1280]{1,0:T(1,128)} %param.10) | copy-start | bytes 15364
  193.8 114.4 %copy-start.3 = (f32[320,1280]{1,0:T(8,128)S(1)}, f32[320,1280]{1,0:T(8,128)}, u32[]{:S(2)}) copy-start(f32[320,1280]{1,0:T(8,128)} %fusion) | copy-start | bytes 4915204
  308.2 10.5 %copy-start = (f32[64,20,1280]{2,1,0:T(8,128)S(1)}, f32[64,20,1280]{2,1,0:T(8,128)}, u32[]{:S(2)}) copy-start(f32[64,20,1280]{2,1,0:T(8,128)} %dot_general.37) | copy-start | bytes 19660804
  333.6 7.0 %copy-start.2 = (f32[1,320,1280]{2,1,0:T(8,128)S(1)}, f32[1,320,1280]{2,1,0:T(8,128)}, u32[]{:S(2)}) copy-start(f32[1,320,1280]{2,1,0:T(8,128)} %copy-done.1) | copy-start | bytes 4915204
  333.6 55.4 %all-to-all-start.3 = ((f32[1,320,64,20]{1,0,3,2:T(1,128)}), f32[1,320,64,20]{1,0,3,2:T(1,128)}, u32[]{:S(2)}, u32[]{:S(2)}) async-start(f32[1,320,64,20]{1,0,3,2:T(1,128)} %copy.22), calls=%async_computation.3 | async-start | bytes 3932160 | tf_op jit(solution)/shard_map/all_to_all | solution.py:45
Sparse Core Ops, SparseCore 0:
  95.9 65.9 all-gather.7
  175.6 132.5 all-gather.9
  310.0 67.2 all-gather.5
